TPU v7x, 32 devices: a whole 2x2x4 slice. The times are simulated.
32 devices in a mesh: slab: 2 (over y), grid: 4 (over z), stack: 4 (over x, core).
Axes of the slice: x: 2, y: 2, z: 4, core: 2. Of those that a mesh axis runs over, the one named last changes fastest.
Arguments:
- disp: float32 [8, 2, 32, 4096], P(('slab', 'stack'), None, 'grid'), parts along dimension 0, may hold values from -6 to 6
- targets: float32 [8, 2, 32, 4096], P(('slab', 'stack'), None, 'grid'), parts along dimension 0, may hold values from -6 to 6
- stiffness: float32 [8], replicated, may hold values from 0.03 to 0.15
- stiff_class: int32 [8, 32, 32], P(('slab', 'stack'), 'grid'), parts along dimension 0, may hold values from 0 to 7
- match_dest: int32 [8, 32, 32], P(('slab', 'stack'), 'grid'), parts along dimension 0, may hold values from -1 to 1023, as said below
Outputs:
- moved: float32 [8, 2, 32, 4096], P(('slab', 'stack'), None, 'grid'), parts along dimension 0
- velocity: float32 [8, 2, 32, 4096], P(('slab', 'stack'), None, 'grid'), parts along dimension 0
There are 2 independent parts, one for each index of `slab`. A program takes and returns all parts, laid end to end along the dimension named above; an argument that names none is the same for every part. Nothing has to cross between parts.
Inputs may be any that keep to these rules, and one draw needn't show every extreme that they name: `match_dest`: each entry is -1 or a block number of the next section; every entry of the last section is -1. From the rows of one grid index, at most 128 blocks are matched into the rows of any one grid index, and in every section but the last some grid index receives exactly 128 from every grid index.
All inputs are finite; a program needn't handle non-finite values.
Results may differ from a plain program's by a relative error of at most 0.00027.
Values sent between devices are 32-bit elements; how exact they have to be, the bound alone decides.
A program may use at most 64 MiB of HBM per device.

v0:
```python
import functools

import jax
import jax.numpy as jnp
from jax import lax
from jax.experimental import pallas as pl
from jax.experimental.pallas import tpu as pltpu
from jax.sharding import Mesh
from jax.sharding import PartitionSpec as P

BLOCK = 128
CLASSES = 8
STEPS = 8


match_gain = 0.1
damping = 0.5


def with_halo(value, sides, width):
    for axis, dim in sides:
        peers, length = (lax.axis_size(axis), value.shape[dim])
        up = [(i, (i + 1) % peers) for i in range(peers - 1)]
        down = [(j, i) for i, j in up]
        last = lax.slice_in_dim(value, length - width, length, axis=dim)
        first = lax.slice_in_dim(value, 0, width, axis=dim)
        before = lax.ppermute(last, axis, up)
        after = lax.ppermute(first, axis, down)
        value = jnp.concatenate([before, value, after], axis=dim)
    return value


def passed_along(value, axis, steps):
    count = lax.axis_size(axis)
    first, last = (max(0, -steps), min(count, count - steps))
    return lax.ppermute(value, axis, [(source, source + steps) for source in range(first, last)])


def laplace(extended):
    padded = jnp.pad(extended, ((0, 0), (0, 0), (1, 1)))
    centre = padded[:, 1:-1, 1:-1]
    edge_sum = (
        padded[:, 2:, 1:-1] + padded[:, :-2, 1:-1] + padded[:, 1:-1, 2:] + padded[:, 1:-1, :-2]
    )
    corner_sum = padded[:, 2:, 2:] + padded[:, 2:, :-2] + padded[:, :-2, 2:] + padded[:, :-2, :-2]
    return edge_sum + 0.5 * corner_sum - 6.0 * centre


def placement(marker, block_count, band_count, capacity):
    alive = marker > 0
    target_block = jnp.maximum(marker - 1, 0)
    band_of = target_block // block_count
    member = ((band_of[:, None] == jnp.arange(band_count)[None, :]) & alive[:, None]).astype(
        jnp.int32
    )
    ranking = jnp.sum(jnp.cumsum(member, axis=0) * member, axis=1) - 1
    slot_of = jnp.where(alive, band_of * capacity + ranking, band_count * capacity)
    local_plus = jnp.where(alive, target_block % block_count + 1, 0)
    slot_total = band_count * capacity
    matching = slot_of[None, :] == jnp.arange(slot_total)[:, None]
    route_matrix = matching.astype(jnp.float32)
    labels = jnp.sum(jnp.where(matching, local_plus[None, :], 0), axis=1)
    return (route_matrix, labels)


def gather_slots(route_matrix, values):
    return jnp.einsum("sb,cbk->csk", route_matrix, values, precision=lax.Precision.HIGHEST)


def spread_slots(route_matrix, values):
    return jnp.einsum("sb,csk->cbk", route_matrix, values, precision=lax.Precision.HIGHEST)


def pack(values, route_matrix, labels, band_count, capacity):
    payload = gather_slots(route_matrix, values)
    return (
        payload.reshape(2, band_count, capacity, BLOCK),
        labels.reshape(1, band_count, capacity),
    )


def settle(blocks, payload, labels):
    block_count = blocks.shape[1]
    flat_payload = payload.reshape(2, -1, BLOCK)
    flat_labels = labels.reshape(-1)
    slot_selector = (flat_labels[:, None] - 1 == jnp.arange(block_count)[None, :]).astype(
        jnp.float32
    )
    alive = (flat_labels > 0).astype(jnp.float32)[None, :, None]
    picked = gather_slots(slot_selector, blocks)
    paired = match_gain * alive * (picked - flat_payload)
    reaction = spread_slots(slot_selector, paired)
    return (paired, reaction)


def per_device(disp, targets, stiffness, stiff_class, match_dest):
    field = disp[0]
    anchor = targets[0]
    row_count = field.shape[1]
    col_count = field.shape[2]
    block_count = row_count * (col_count // BLOCK)
    band_count = lax.axis_size("grid")
    capacity = max(2, 2 * block_count // band_count)
    member = (stiff_class[0][..., None] == jnp.arange(CLASSES)).astype(jnp.float32)
    kappa = jnp.repeat(jnp.sum(member * stiffness, axis=-1), BLOCK, axis=-1)
    marker = match_dest[0].reshape(block_count) + 1
    own_matrix, own_labels = placement(marker, block_count, band_count, capacity)
    velocity = jnp.zeros_like(field)
    for repeat_index in range(STEPS):
        extended = with_halo(field, (("grid", 1),), 1)
        blocks = field.reshape(2, block_count, BLOCK)
        pulled = (field - anchor).reshape(2, block_count, BLOCK)
        payload, labels = pack(pulled, own_matrix, own_labels, band_count, capacity)
        moved_payload, moved_labels = (
            lax.all_to_all(payload, "grid", split_axis=1, concat_axis=1, tiled=True),
            lax.all_to_all(labels, "grid", split_axis=1, concat_axis=1, tiled=True),
        )
        held_payload, held_labels = passed_along((moved_payload, moved_labels), "stack", 1)
        paired, reaction = settle(blocks, held_payload, held_labels)
        returned = passed_along(paired.reshape(2, band_count, capacity, BLOCK), "stack", -1)
        arrived = lax.all_to_all(returned, "grid", split_axis=1, concat_axis=1, tiled=True)
        gained = spread_slots(own_matrix, arrived.reshape(2, -1, BLOCK))
        match_force = (gained - reaction).reshape(2, row_count, col_count)
        velocity = damping * velocity + kappa * laplace(extended) + match_force
        field = field + velocity
    return (field[None], velocity[None])


TILE = 8
BAND = 256
VMEM_BYTES = 58 * 1024 * 1024


def two_pieces(value):
    high = value.astype(jnp.bfloat16)
    low = (value - high.astype(jnp.float32)).astype(jnp.bfloat16)
    return jnp.concatenate([high, low], axis=1)


def joined(pieces):
    return pieces[:, :BLOCK] + pieces[:, BLOCK:]


def relax_kernel(
    sections,
    bands,
    place_ref,
    data_ref,
    kappa_ref,
    dest_ref,
    dest_row_ref,
    out_ref,
    pick_ref,
    drop_ref,
    field_ref,
    velocity_ref,
    weight_ref,
    force_ref,
    pieces_ref,
    spread_ref,
    match_ref,
):
    total = bands * BAND
    lane = lax.broadcasted_iota(jnp.int32, (TILE, BLOCK), 1)
    sub = lax.broadcasted_iota(jnp.int32, (TILE, BLOCK), 0)
    section = place_ref[0]
    half = place_ref[1]

    def start_of(s, band):
        return data_ref[(band // 2) * sections + s, band % 2, 0]

    def target_of(s, band):
        return data_ref[(band // 2) * sections + s, band % 2, 1]

    def spread_band(slot, s, band):
        for k in range(BAND // TILE):
            centre = field_ref[s, band, k + 1]
            before = field_ref[s, band, k]
            after = field_ref[s, band, k + 2]
            left = pltpu.roll(jnp.where(lane == BLOCK - 1, before, centre), 1, 1)
            right = pltpu.roll(jnp.where(lane == 0, after, centre), BLOCK - 1, 1)
            spread_ref[slot, s, band + 1, k] = centre + 0.5 * (left + right)

    wide = lax.broadcasted_iota(jnp.int32, (BAND, BLOCK), 1)
    tall = lax.broadcasted_iota(jnp.int32, (BAND, BLOCK), 0)

    def build(band, carry):
        rows = pl.ds(pl.multiple_of(band * BAND, BAND), BAND)
        for s in range(sections - 1):
            dest = dest_ref[s, rows]
            for j in range(total // BLOCK):
                cols = slice(j * BLOCK, (j + 1) * BLOCK)
                hit = dest == wide + j * BLOCK
                pick_ref[s, rows, cols] = jnp.where(hit, 1.0, 0.0).astype(jnp.bfloat16)
                hit = dest_row_ref[s, :, cols] == tall + band * BAND
                drop_ref[s, rows, cols] = jnp.where(hit, 1.0, 0.0).astype(jnp.bfloat16)
        return carry

    lax.fori_loop(0, bands, build, 0)

    edge = jnp.zeros((BAND // TILE, TILE, BLOCK), jnp.float32)
    for s in range(sections):
        for slot in range(2):
            spread_ref[slot, s, 0] = edge
            spread_ref[slot, s, bands + 1] = edge

    def begin(band, carry):
        rows = pl.ds(pl.multiple_of(band * BAND, BAND), BAND)
        for s in range(sections):
            field_ref[s, band, 0] = edge[0]
            field_ref[s, band, BAND // TILE + 1] = edge[0]
            value = start_of(s, band)
            field_ref[s, band, 1 : BAND // TILE + 1] = value.reshape(BAND // TILE, TILE, BLOCK)
            pieces_ref[0, s, rows] = two_pieces(value)
            pieces_ref[1, s, rows] = two_pieces(target_of(s, band))
            velocity_ref[s, rows] = jnp.zeros((BAND, BLOCK), jnp.float32)
            spread_band(0, s, band)
        return carry

    lax.fori_loop(0, bands, begin, 0)

    ones = jnp.ones((total, BLOCK), jnp.bfloat16)

    def constants(band, carry):
        rows = pl.ds(pl.multiple_of(band * BAND, BAND), BAND)
        for s in range(sections):
            weight = 8.0 * kappa_ref[s, rows]
            force = jnp.zeros((BAND, BLOCK), jnp.float32)
            if s < sections - 1:
                alive = jnp.where(dest_ref[s, rows] >= 0, match_gain, 0.0)
                weight = weight + alive
                force = force + alive * target_of(s, band)
            if s > 0:
                drop = drop_ref[s - 1, rows]
                count = jnp.dot(drop, ones, preferred_element_type=jnp.float32)
                moved = jnp.dot(drop, pieces_ref[1, s - 1], preferred_element_type=jnp.float32)
                weight = weight + match_gain * count
                force = force - match_gain * joined(moved)
            weight_ref[s, rows] = weight
            force_ref[s, rows] = force
        return carry

    lax.fori_loop(0, bands, constants, 0)

    def step(t, carry):
        now = lax.rem(t, 2)
        later = 1 - now

        def one_section(s):
            def one_band(band, inner):
                rows = pl.ds(pl.multiple_of(band * BAND, BAND), BAND)
                sums = None
                if s < sections - 1:
                    sums = jnp.dot(
                        pick_ref[s, rows], pieces_ref[now, s + 1], preferred_element_type=jnp.float32
                    )
                if s > 0:
                    other = jnp.dot(
                        drop_ref[s - 1, rows],
                        pieces_ref[now, s - 1],
                        preferred_element_type=jnp.float32,
                    )
                    sums = other if sums is None else sums + other
                match_ref[...] = joined(sums)
                base = pl.multiple_of(band * BAND, BAND)
                for k in range(0, BAND // TILE, 2):
                    pair = []
                    for q in (k, k + 1):
                        spot = pl.ds(base + q * TILE, TILE)
                        here = spread_ref[now, s, band + 1, q]
                        above = spread_ref[now, s, band, q]
                        below = spread_ref[now, s, band + 2, q]
                        up = pltpu.roll(jnp.where(sub == TILE - 1, above, here), 1, 0)
                        down = pltpu.roll(jnp.where(sub == 0, below, here), TILE - 1, 0)
                        field = field_ref[s, band, q + 1]
                        velocity = (
                            damping * velocity_ref[s, spot]
                            + kappa_ref[s, spot] * (2.0 * here + up + down)
                            - weight_ref[s, spot] * field
                            + match_gain * match_ref[q * TILE : (q + 1) * TILE]
                            + force_ref[s, spot]
                        )
                        field = field + velocity
                        velocity_ref[s, spot] = velocity
                        field_ref[s, band, q + 1] = field
                        pair.append(field)
                    spot = pl.ds(base + k * TILE, 2 * TILE)
                    pieces_ref[later, s, spot] = two_pieces(jnp.concatenate(pair, axis=0))
                spread_band(later, s, band)
                return inner

            lax.fori_loop(0, bands, one_band, 0)

        for s in range(sections):
            distance = jnp.abs(section - s)

            @pl.when(distance <= STEPS - 1 - t)
            def _(s=s):
                one_section(s)

        return carry

    lax.fori_loop(0, STEPS, step, 0)
    for q in range(2):
        band = half * 2 + q
        out_ref[q, 0] = field_ref[section, band, 1 : BAND // TILE + 1].reshape(BAND, BLOCK)
        out_ref[q, 1] = velocity_ref[section, pl.ds(pl.multiple_of(band * BAND, BAND), BAND)]


def tiled_order(value):
    lead = value.shape[:-2]
    rows, cols = value.shape[-2:]
    split = value.reshape(*lead, rows, cols // BLOCK, BLOCK)
    return jnp.swapaxes(split, -3, -2).reshape(*lead, rows * (cols // BLOCK), BLOCK)


def whole_component(disp, targets, stiffness, stiff_class, match_dest):
    sections = lax.axis_size("stack")
    bands = lax.axis_size("half") * 2
    blocks_row = stiff_class.shape[-1]
    both = tiled_order(jnp.stack([disp[0], targets[0]], axis=1))
    both = lax.all_to_all(both, "comp", split_axis=0, concat_axis=0, tiled=True)
    data = lax.all_gather(both, ("half", "stack"))
    small = jnp.concatenate([stiff_class, match_dest])
    small = lax.all_gather(small, ("half", "comp", "stack"))
    small = small.reshape(bands, sections, 2, TILE, blocks_row).transpose(2, 1, 0, 4, 3)
    small = small.reshape(2, sections, bands * BAND)
    member = (small[0][..., None] == jnp.arange(CLASSES)).astype(jnp.float32)
    kappa = jnp.sum(member * stiffness, axis=-1)
    dest = small[1][: sections - 1]
    row, col = dest // blocks_row, dest % blocks_row
    dest = jnp.where(dest >= 0, (row // TILE) * BAND + col * TILE + row % TILE, -1)
    total = bands * BAND
    kappa_wide = jnp.broadcast_to(kappa[..., None], (sections, total, BLOCK))
    dest_wide = jnp.broadcast_to(dest[..., None], (sections - 1, total, BLOCK))
    place = jnp.stack([lax.axis_index("stack"), lax.axis_index("half")]).astype(jnp.int32)
    tiles = BAND // TILE
    result = pl.pallas_call(
        functools.partial(relax_kernel, sections, bands),
        out_shape=jax.ShapeDtypeStruct((2, 2, BAND, BLOCK), jnp.float32),
        in_specs=[pl.BlockSpec(memory_space=pltpu.SMEM)]
        + [pl.BlockSpec(memory_space=pltpu.VMEM)] * 4,
        out_specs=pl.BlockSpec(memory_space=pltpu.VMEM),
        scratch_shapes=[
            pltpu.VMEM((sections - 1, total, total), jnp.bfloat16),
            pltpu.VMEM((sections - 1, total, total), jnp.bfloat16),
            pltpu.VMEM((sections, bands, tiles + 2, TILE, BLOCK), jnp.float32),
            pltpu.VMEM((sections, total, BLOCK), jnp.float32),
            pltpu.VMEM((sections, total, BLOCK), jnp.float32),
            pltpu.VMEM((sections, total, BLOCK), jnp.float32),
            pltpu.VMEM((2, sections, total, 2 * BLOCK), jnp.bfloat16),
            pltpu.VMEM((2, sections, bands + 2, tiles, TILE, BLOCK), jnp.float32),
            pltpu.VMEM((BAND, BLOCK), jnp.float32),
        ],
        compiler_params=pltpu.CompilerParams(vmem_limit_bytes=VMEM_BYTES),
    )(place, data, kappa_wide, dest_wide, dest[:, None, :])
    result = lax.all_to_all(result, "comp", split_axis=0, concat_axis=0, tiled=True)
    result = result.reshape(2, 2, tiles, TILE, BLOCK).transpose(1, 0, 3, 2, 4)
    result = result.reshape(2, 1, 2, TILE, tiles * BLOCK)
    return (result[0], result[1])


def solution(mesh):
    by_name = mesh.shape
    if by_name["grid"] % 2 == 0 and by_name["grid"] <= 4 and by_name["stack"] <= 4:
        inner = Mesh(
            mesh.devices.reshape(by_name["slab"], by_name["grid"] // 2, 2, by_name["stack"]),
            ("slab", "half", "comp", "stack"),
        )
        body, grid = whole_component, ("half", "comp")
    else:
        inner, body, grid = mesh, per_device, "grid"
    return jax.shard_map(
        body,
        mesh=inner,
        in_specs=(
            P(("slab", "stack"), None, grid, None),
            P(("slab", "stack"), None, grid, None),
            P(),
            P(("slab", "stack"), grid, None),
            P(("slab", "stack"), grid, None),
        ),
        out_specs=(
            P(("slab", "stack"), None, grid, None),
            P(("slab", "stack"), None, grid, None),
        ),
        check_vma=False,
    )
```

profile of v0, /device:TPU:0, one launch (start us, length us, event | category | flops | bytes accessed | tf_op | source)
XLA Modules:
  0.0 158.5 jit_solution(658485308364028490)
XLA Ops:
  7.2 0.0 copy-start
  7.2 0.0 copy-start.1
  7.2 0.0 all-gather.4.cloned.1.call-start
  7.2 1.1 maximum_bitcast_fusion
  8.3 0.0 copy-start.2
  8.3 12.7 %all_to_all.10 = f32[2,2,256,128]{3,2,1,0:T(8,128)} all-to-all(f32[2,2,256,128]{3,2,1,0:T(8,128)S(1)} %maximum_bitcast_fusion), channel_id=1, replica_groups=mesh['slab'=2,'half'=2,'comp'=2,'stack'=4] {'comp'}, dimensions={0} | all-to-all | bytes 1048576 | tf_op jit(solution)/shard_map/all_to_all | solution.py:322
  21.0 0.0 all-gather.4.cloned.1.call-update
  21.0 0.0 copy-done
  21.1 0.0 copy-done.1
  21.1 21.2 %all-gather.1 = s32[32,8,32]{2,1,0:T(8,128)S(1)} all-gather(s32[2,8,32]{2,1,0:T(8,128)S(1)} %pad_add_fusion), channel_id=3, replica_groups=mesh['slab'=2,'half'=2,'comp'=2,'stack'=4] {'half','comp','stack'}, dimensions={0}, use_global_device_ids=true | all-gather | bytes 34816 | tf_op jit(solution)/shard_map/all_gather | solution.py:325
  42.3 0.2 copy.16
  42.6 0.1 slice.26
  42.7 0.1 slice.25
  42.9 0.2 eq.18
  43.0 0.7 pad_add_fusion.1.place_ref
  43.7 0.0 copy-done.2
  43.7 0.1 select_reduce_fusion
  43.8 0.8 compare_select_fusion.dest_row_ref
  44.6 0.1 fusion.3
  44.7 31.6 %all-gather.4.cloned.1.call-done = f32[16,2,256,128]{3,2,1,0:T(8,128)} async-done(((f32[2,2,256,128]{3,2,1,0:T(8,128)}), f32[16,2,256,128]{3,2,1,0:T(8,128)}) %all-gather.4.cloned.1.call-update) | async-done | bytes 4194320 | tf_op jit(solution)/shard_map/all_gather | solution.py:323
  76.3 1.5 broadcast_in_dim.7.dest_ref
  77.7 1.9 %broadcast_in_dim.6.kappa_ref = f32[4,1024,128]{2,1,0:T(8,128)} broadcast(f32[4,1024]{1,0:T(4,128)S(1)} %select_reduce_fusion), dimensions={0,1} | broadcast | bytes 2113536 | tf_op jit(solution)/shard_map/broadcast_in_dim | solution.py:334
  79.7 61.2 %shard_map.68 = f32[2,2,256,128]{3,2,1,0:T(8,128)} custom-call(s32[2]{0:T(128)} %pad_add_fusion.1.place_ref, f32[8,2,2,256,128]{4,3,2,1,0:T(8,128)} %bitcast.34, f32[4,1024,128]{2,1,0:T(8,128)} %broadcast_in_dim.6.kappa_ref, s32[3,1024,128]{2,1,0:T(8,128)} %broadcast_in_dim.7.dest_ref, s32[3,1,1024]{2,1,0:T(1,128)} %compare_select_fusion.dest_row_ref), custom_call_target="tpu_custom_call" | custom-call | tf_op jit(solution)/shard_map/pallas_call | solution.py:338
  140.8 10.1 %all_to_all.11 = f32[2,2,256,128]{3,2,1,0:T(8,128)S(1)} all-to-all(f32[2,2,256,128]{3,2,1,0:T(8,128)} %shard_map.68), channel_id=1, replica_groups=mesh['slab'=2,'half'=2,'comp'=2,'stack'=4] {'comp'}, dimensions={0} | all-to-all | bytes 1048576 | tf_op jit(solution)/shard_map/all_to_all | solution.py:357
  150.9 0.8 slice_bitcast_fusion
  (3 shorter events, 0.0 us)
Async XLA Ops:
  7.2 13.9 %copy-start = (s32[1,8,32]{2,1,0:T(8,128)S(1)}, s32[1,8,32]{2,1,0:T(8,128)}, u32[]{:S(2)}) copy-start(s32[1,8,32]{2,1,0:T(8,128)} %param.9) | copy-start | bytes 3076
  7.2 13.9 %copy-start.1 = (s32[1,8,32]{2,1,0:T(8,128)S(1)}, s32[1,8,32]{2,1,0:T(8,128)}, u32[]{:S(2)}) copy-start(s32[1,8,32]{2,1,0:T(8,128)} %param.8) | copy-start | bytes 3076
  7.2 69.1 %all-gather.4.cloned.1.call-start = ((), (), s32[]{:S(2)}) async-start(), calls=%async_computation.2 | async-start | bytes 4718592 | tf_op jit(solution)/shard_map/all_gather | solution.py:323
  8.3 35.4 %copy-start.2 = (f32[8]{0:T(128)S(1)}, f32[8]{0:T(128)}, u32[]{:S(2)}) copy-start(f32[8]{0:T(128)} %param.7) | copy-start | bytes 100
Sparse Core Ops, SparseCore 0:
  21.2 55.0 all-gather.3
where the time goes:
time: 162 us; the launch traced here: 159 us
  Pallas kernels  61.2 us (38%)
  blocking collectives  44 us (27%)
  waiting for transfers between devices  31.6 us (20%)
  between operations  14.1 us (9%)
  local copies, waits for them, and re-layouts  4.92 us (3%)
  other arithmetic  2.7 us (2%)
    pallas_call x1, Pallas kernels, whole_component(): pl.pallas_call(functools.partial(relax_kernel, sections, bands), out_shap...  61.2 us
    all_gather x1, waiting for transfers between devices, whole_component(): data = lax.all_gather(both, ('half', 'stack'))  31.6 us
    all_gather x1, blocking collectives, whole_component(): small = lax.all_gather(small, ('half', 'comp', 'stack'))  21.2 us
    all_to_all x1, blocking collectives, whole_component(): both = lax.all_to_all(both, 'comp', split_axis=0, concat_axis=0, tiled=True)  12.7 us
    all_to_all x1, blocking collectives, whole_component(): lax.all_to_all(result, 'comp', split_axis=0, concat_axis=0, tiled=True)  10.1 us
  transfers between devices with their start and end apart: 1, of which 1 were waited for; matrix products, arithmetic and copies ran while one was open for 1% of the time, Pallas kernels for 0%

commit v1 on v0

--- a/solution.py
+++ b/solution.py
@@ -146,10 +146,9 @@
     bands,
     place_ref,
     data_ref,
+    out_ref,
     kappa_ref,
     dest_ref,
-    dest_row_ref,
-    out_ref,
     pick_ref,
     drop_ref,
     field_ref,
@@ -167,10 +166,24 @@
     half = place_ref[1]
 
     def start_of(s, band):
-        return data_ref[(band // 2) * sections + s, band % 2, 0]
+        return data_ref[s // 2, s % 2, band, 0, 0:BAND]
 
     def target_of(s, band):
-        return data_ref[(band // 2) * sections + s, band % 2, 1]
+        return data_ref[s // 2, s % 2, band, 1, 0:BAND]
+
+    def constant_row(s, which, j):
+        line = BAND + 2 * which + j % 2
+        return data_ref[s // 2, s % 2, j // 2, 0, line : line + 1]
+
+    def as_column(row):
+        return jnp.broadcast_to(row, (BLOCK, BLOCK)).T
+
+    for s in range(sections):
+        for j in range(total // BLOCK):
+            spot = slice(j * BLOCK, (j + 1) * BLOCK)
+            kappa_ref[s, spot] = as_column(constant_row(s, 0, j))
+            if s < sections - 1:
+                dest_ref[s, spot] = as_column(constant_row(s, 1, j)).astype(jnp.int32)
 
     def spread_band(slot, s, band):
         for k in range(BAND // TILE):
@@ -192,7 +205,7 @@
                 cols = slice(j * BLOCK, (j + 1) * BLOCK)
                 hit = dest == wide + j * BLOCK
                 pick_ref[s, rows, cols] = jnp.where(hit, 1.0, 0.0).astype(jnp.bfloat16)
-                hit = dest_row_ref[s, :, cols] == tall + band * BAND
+                hit = constant_row(s, 1, j).astype(jnp.int32) == tall + band * BAND
                 drop_ref[s, rows, cols] = jnp.where(hit, 1.0, 0.0).astype(jnp.bfloat16)
         return carry
 
@@ -314,34 +327,130 @@
     return jnp.swapaxes(split, -3, -2).reshape(*lead, rows * (cols // BLOCK), BLOCK)
 
 
+def gather_kernel(bands, own_ref, data_ref, local_sem, send_sem, recv_sem):
+    half, comp, stack = (lax.axis_index(name) for name in ("half", "comp", "stack"))
+    slab = lax.axis_index("slab")
+    z = half * 2 + comp
+    x, core = stack // 2, stack % 2
+
+    def device(to_x, to_core, to_z):
+        return (slab, to_z // 2, to_z % 2, to_x * 2 + to_core)
+
+    along = [lax.rem(z + j, bands) for j in range(bands)]
+    over_x = device(1 - x, core, z)
+    sibling = device(x, 1 - core, z)
+    barrier = pltpu.get_barrier_semaphore()
+    for peer in [device(x, core, to_z) for to_z in along[1:]] + [over_x, sibling]:
+        pl.semaphore_signal(barrier, inc=1, device_id=peer, device_id_type=pl.DeviceIdType.MESH)
+    pl.semaphore_wait(barrier, bands + 1)
+
+    started = []
+
+    def send(source, slot, kind, peer):
+        copy = pltpu.make_async_remote_copy(
+            src_ref=source,
+            dst_ref=data_ref.at[slot],
+            send_sem=send_sem.at[len(started)],
+            recv_sem=recv_sem.at[slot],
+            device_id=peer,
+            device_id_type=pl.DeviceIdType.MESH,
+        )
+        copy.start()
+        started.append(copy)
+
+    def arrive(slot):
+        pltpu.make_async_remote_copy(
+            src_ref=data_ref.at[slot],
+            dst_ref=data_ref.at[slot],
+            send_sem=send_sem.at[0],
+            recv_sem=recv_sem.at[slot],
+            device_id=sibling,
+            device_id_type=pl.DeviceIdType.MESH,
+        ).wait_recv()
+
+    for kind in range(2):
+        for to_z in along[1:]:
+            send(own_ref.at[to_z % 2, kind], (x, core, z, kind), kind, device(x, core, to_z))
+        send(own_ref.at[comp, kind], (x, core, z, kind), kind, over_x)
+        send(own_ref.at[comp, kind], (x, core, z, kind), kind, sibling)
+        keep = pltpu.make_async_copy(
+            own_ref.at[comp, kind], data_ref.at[x, core, z, kind], local_sem.at[kind]
+        )
+        keep.start()
+    for kind in range(2):
+        for band in along[1:]:
+            slot = (x, core, band, kind)
+            arrive(slot)
+            send(data_ref.at[slot], slot, kind, over_x)
+            send(data_ref.at[slot], slot, kind, sibling)
+        for band in along:
+            slot = (1 - x, core, band, kind)
+            arrive(slot)
+            send(data_ref.at[slot], slot, kind, sibling)
+    for kind in range(2):
+        for band in along:
+            for from_x in range(2):
+                arrive((from_x, 1 - core, band, kind))
+    for copy in started:
+        copy.wait_send()
+    for kind in range(2):
+        pltpu.make_async_copy(
+            own_ref.at[comp, kind], data_ref.at[x, core, z, kind], local_sem.at[kind]
+        ).wait()
+
+
+def tiled_order(value):
+    lead = value.shape[:-2]
+    rows, cols = value.shape[-2:]
+    split = value.reshape(*lead, rows, cols // BLOCK, BLOCK)
+    return jnp.swapaxes(split, -3, -2).reshape(*lead, rows * (cols // BLOCK), BLOCK)
+
+
 def whole_component(disp, targets, stiffness, stiff_class, match_dest):
     sections = lax.axis_size("stack")
     bands = lax.axis_size("half") * 2
     blocks_row = stiff_class.shape[-1]
-    both = tiled_order(jnp.stack([disp[0], targets[0]], axis=1))
-    both = lax.all_to_all(both, "comp", split_axis=0, concat_axis=0, tiled=True)
-    data = lax.all_gather(both, ("half", "stack"))
-    small = jnp.concatenate([stiff_class, match_dest])
-    small = lax.all_gather(small, ("half", "comp", "stack"))
-    small = small.reshape(bands, sections, 2, TILE, blocks_row).transpose(2, 1, 0, 4, 3)
-    small = small.reshape(2, sections, bands * BAND)
-    member = (small[0][..., None] == jnp.arange(CLASSES)).astype(jnp.float32)
+    total = bands * BAND
+    tiles = BAND // TILE
+    member = (stiff_class[0][..., None] == jnp.arange(CLASSES)).astype(jnp.float32)
     kappa = jnp.sum(member * stiffness, axis=-1)
-    dest = small[1][: sections - 1]
+    dest = match_dest[0]
     row, col = dest // blocks_row, dest % blocks_row
     dest = jnp.where(dest >= 0, (row // TILE) * BAND + col * TILE + row % TILE, -1)
-    total = bands * BAND
-    kappa_wide = jnp.broadcast_to(kappa[..., None], (sections, total, BLOCK))
-    dest_wide = jnp.broadcast_to(dest[..., None], (sections - 1, total, BLOCK))
+    constants = jnp.stack([kappa.T, dest.astype(jnp.float32).T]).reshape(4, BLOCK)
+    constants = jnp.pad(constants, ((0, TILE - 4), (0, 0)))
+    both = tiled_order(jnp.stack([disp[0], targets[0]], axis=1))
+    extra = jnp.broadcast_to(constants, (2, 2, TILE, BLOCK))
+    both = jnp.concatenate([both, extra], axis=2)
+    copies = 2 * (bands + 1) + 2 * (2 * (bands - 1) + bands)
+    data = pl.pallas_call(
+        functools.partial(gather_kernel, bands),
+        out_shape=jax.ShapeDtypeStruct(
+            (sections // 2, 2, bands, 2, BAND + TILE, BLOCK), jnp.float32
+        ),
+        in_specs=[pl.BlockSpec(memory_space=pltpu.VMEM)],
+        out_specs=pl.BlockSpec(memory_space=pltpu.VMEM),
+        scratch_shapes=[
+            pltpu.SemaphoreType.DMA((2,)),
+            pltpu.SemaphoreType.DMA((copies,)),
+            pltpu.SemaphoreType.DMA((sections // 2, 2, bands, 2)),
+        ],
+        compiler_params=pltpu.CompilerParams(
+            collective_id=0, has_side_effects=True, vmem_limit_bytes=16 * 1024 * 1024
+        ),
+    )(both)
     place = jnp.stack([lax.axis_index("stack"), lax.axis_index("half")]).astype(jnp.int32)
-    tiles = BAND // TILE
     result = pl.pallas_call(
         functools.partial(relax_kernel, sections, bands),
         out_shape=jax.ShapeDtypeStruct((2, 2, BAND, BLOCK), jnp.float32),
-        in_specs=[pl.BlockSpec(memory_space=pltpu.SMEM)]
-        + [pl.BlockSpec(memory_space=pltpu.VMEM)] * 4,
+        in_specs=[
+            pl.BlockSpec(memory_space=pltpu.SMEM),
+            pl.BlockSpec(memory_space=pltpu.VMEM),
+        ],
         out_specs=pl.BlockSpec(memory_space=pltpu.VMEM),
         scratch_shapes=[
+            pltpu.VMEM((sections, total, BLOCK), jnp.float32),
+            pltpu.VMEM((sections - 1, total, BLOCK), jnp.int32),
             pltpu.VMEM((sections - 1, total, total), jnp.bfloat16),
             pltpu.VMEM((sections - 1, total, total), jnp.bfloat16),
             pltpu.VMEM((sections, bands, tiles + 2, TILE, BLOCK), jnp.float32),
@@ -353,7 +462,7 @@
             pltpu.VMEM((BAND, BLOCK), jnp.float32),
         ],
         compiler_params=pltpu.CompilerParams(vmem_limit_bytes=VMEM_BYTES),
-    )(place, data, kappa_wide, dest_wide, dest[:, None, :])
+    )(place, data)
     result = lax.all_to_all(result, "comp", split_axis=0, concat_axis=0, tiled=True)
     result = result.reshape(2, 2, tiles, TILE, BLOCK).transpose(1, 0, 3, 2, 4)
     result = result.reshape(2, 1, 2, TILE, tiles * BLOCK)
@@ -362,7 +471,7 @@
 
 def solution(mesh):
     by_name = mesh.shape
-    if by_name["grid"] % 2 == 0 and by_name["grid"] <= 4 and by_name["stack"] <= 4:
+    if by_name["grid"] % 2 == 0 and by_name["grid"] <= 4 and by_name["stack"] == 4:
         inner = Mesh(
             mesh.devices.reshape(by_name["slab"], by_name["grid"] // 2, 2, by_name["stack"]),
             ("slab", "half", "comp", "stack"),

time: 162 us -> 125 us (0.77)
  the two profiles are of different devices: /device:TPU:0 before, /device:TPU:1 now
where the time goes in v1:
time: 125 us; the launch traced here: 124 us
  Pallas kernels  102 us (82%)
  blocking collectives  15.4 us (12%)
  other arithmetic  3.26 us (3%)
  local copies, waits for them, and re-layouts  2.98 us (2%)
    pallas_call x1, Pallas kernels, whole_component(): pl.pallas_call(functools.partial(relax_kernel, sections, bands), out_shap...  65.2 us
    pallas_call x1, Pallas kernels, whole_component(): pl.pallas_call(functools.partial(gather_kernel, bands), out_shape=jax.Sha...  36.7 us
    all_to_all x1, blocking collectives, whole_component(): lax.all_to_all(result, 'comp', split_axis=0, concat_axis=0, tiled=True)  15.4 us

profile of v1, /device:TPU:1, one launch (start us, length us, event | category | flops | bytes accessed | tf_op | source)
XLA Modules:
  0.0 124.3 jit_solution(2038513909219363347)
XLA Ops:
  0.6 0.7 fusion.5
  1.3 0.8 select_reduce_fusion
  2.1 0.1 copy.14
  2.2 0.1 reshape.26
  2.3 1.1 maximum_bitcast_fusion
  3.5 36.7 %shard_map.68.data_ref = f32[2,2,4,2,264,128]{5,4,3,2,1,0:T(8,128)S(1)} custom-call(f32[2,2,264,128]{3,2,1,0:T(8,128)S(1)} %pad_maximum_fusion.own_ref), custom_call_target="tpu_custom_call" | custom-call | tf_op jit(solution)/shard_map/pallas_call | solution.py:426
  40.2 0.0 copy-start
  40.2 2.0 %copy-done = f32[2,2,4,2,264,128]{5,4,3,2,1,0:T(8,128)} copy-done((f32[2,2,4,2,264,128]{5,4,3,2,1,0:T(8,128)}, f32[2,2,4,2,264,128]{5,4,3,2,1,0:T(8,128)S(1)}, u32[]{:S(2)}) %copy-start) | copy-done | bytes 4325400
  42.2 0.7 pad_add_fusion.place_ref
  42.8 65.2 %shard_map.69 = f32[2,2,256,128]{3,2,1,0:T(8,128)} custom-call(s32[2]{0:T(128)} %pad_add_fusion.place_ref, f32[2,2,4,2,264,128]{5,4,3,2,1,0:T(8,128)} %copy-done), custom_call_target="tpu_custom_call" | custom-call | tf_op jit(solution)/shard_map/pallas_call | solution.py:443
  108.1 15.4 %all_to_all.5 = f32[2,2,256,128]{3,2,1,0:T(8,128)S(1)} all-to-all(f32[2,2,256,128]{3,2,1,0:T(8,128)} %shard_map.69), channel_id=1, replica_groups=mesh['slab'=2,'half'=2,'comp'=2,'stack'=4] {'comp'}, dimensions={0} | all-to-all | bytes 1048576 | tf_op jit(solution)/shard_map/all_to_all | solution.py:466
  123.5 0.8 slice_bitcast_fusion
  (4 shorter events, 0.1 us)
Async XLA Ops:
  40.2 2.0 %copy-start = (f32[2,2,4,2,264,128]{5,4,3,2,1,0:T(8,128)}, f32[2,2,4,2,264,128]{5,4,3,2,1,0:T(8,128)S(1)}, u32[]{:S(2)}) copy-start(f32[2,2,4,2,264,128]{5,4,3,2,1,0:T(8,128)S(1)} %shard_map.68.data_ref) | copy-start | bytes 12976132

commit v2 on v1

--- a/solution.py
+++ b/solution.py
@@ -142,51 +142,64 @@
 
 
 def relax_kernel(
-    sections,
     bands,
-    place_ref,
     data_ref,
     out_ref,
     kappa_ref,
-    dest_ref,
-    pick_ref,
-    drop_ref,
+    out_of_inner_ref,
+    in_of_outer_ref,
+    in_of_far_ref,
     field_ref,
     velocity_ref,
     weight_ref,
     force_ref,
     pieces_ref,
+    far_pieces_ref,
+    far_ref,
     spread_ref,
     match_ref,
+    swap_send,
+    swap_recv,
+    out_send,
+    out_recv,
+    out_local,
 ):
     total = bands * BAND
+    tiles = BAND // TILE
+    slab = lax.axis_index("slab")
+    half, comp, stack = (lax.axis_index(name) for name in ("half", "comp", "stack"))
+    z = half * 2 + comp
+    other_z = half * 2 + 1 - comp
+    x, core = stack // 2, stack % 2
+    sections = (3 * core, 1 + core)
+    far = 2 - core
+    edge_source = 2 * core
+    sibling = (slab, half, comp, x * 2 + 1 - core)
+    beside = (slab, half, 1 - comp, x * 2 + core)
+    across = (slab, half, 1 - comp, x * 2 + 1 - core)
+    barrier = pltpu.get_barrier_semaphore()
+    for peer in (sibling, beside, across):
+        pl.semaphore_signal(barrier, inc=1, device_id=peer, device_id_type=pl.DeviceIdType.MESH)
+    pl.semaphore_wait(barrier, 3)
+
     lane = lax.broadcasted_iota(jnp.int32, (TILE, BLOCK), 1)
     sub = lax.broadcasted_iota(jnp.int32, (TILE, BLOCK), 0)
-    section = place_ref[0]
-    half = place_ref[1]
-
-    def start_of(s, band):
-        return data_ref[s // 2, s % 2, band, 0, 0:BAND]
-
-    def target_of(s, band):
-        return data_ref[s // 2, s % 2, band, 1, 0:BAND]
-
-    def constant_row(s, which, j):
-        line = BAND + 2 * which + j % 2
-        return data_ref[s // 2, s % 2, j // 2, 0, line : line + 1]
+
+    def loaded(s, band, kind):
+        return data_ref[s // 2, s % 2, band, kind, 0:BAND]
+
+    def constant_row(s, which, band, part):
+        line = BAND + 2 * which + part
+        return data_ref[s // 2, s % 2, band, 0, line : line + 1]
 
     def as_column(row):
         return jnp.broadcast_to(row, (BLOCK, BLOCK)).T
 
-    for s in range(sections):
-        for j in range(total // BLOCK):
-            spot = slice(j * BLOCK, (j + 1) * BLOCK)
-            kappa_ref[s, spot] = as_column(constant_row(s, 0, j))
-            if s < sections - 1:
-                dest_ref[s, spot] = as_column(constant_row(s, 1, j)).astype(jnp.int32)
+    def rows_of(band):
+        return pl.ds(pl.multiple_of(band * BAND, BAND), BAND)
 
     def spread_band(slot, s, band):
-        for k in range(BAND // TILE):
+        for k in range(tiles):
             centre = field_ref[s, band, k + 1]
             before = field_ref[s, band, k]
             after = field_ref[s, band, k + 2]
@@ -194,137 +207,232 @@
             right = pltpu.roll(jnp.where(lane == 0, after, centre), BLOCK - 1, 1)
             spread_ref[slot, s, band + 1, k] = centre + 0.5 * (left + right)
 
-    wide = lax.broadcasted_iota(jnp.int32, (BAND, BLOCK), 1)
-    tall = lax.broadcasted_iota(jnp.int32, (BAND, BLOCK), 0)
+    wide = lax.broadcasted_iota(jnp.int32, (BLOCK, BLOCK), 1).astype(jnp.float32)
+    tall = lax.broadcasted_iota(jnp.int32, (BLOCK, BLOCK), 0).astype(jnp.float32)
+    first = core == 0
 
     def build(band, carry):
-        rows = pl.ds(pl.multiple_of(band * BAND, BAND), BAND)
-        for s in range(sections - 1):
-            dest = dest_ref[s, rows]
+        for part in range(2):
+            base = band * BAND + part * BLOCK
+            rows = pl.ds(pl.multiple_of(base, BLOCK), BLOCK)
+            here = tall + base.astype(jnp.float32)
+            for s in range(2):
+                kappa_ref[s, rows] = as_column(constant_row(sections[s], 0, band, part))
+            edge_column = as_column(constant_row(edge_source, 1, band, part))
+            middle_column = as_column(constant_row(1, 1, band, part))
             for j in range(total // BLOCK):
                 cols = slice(j * BLOCK, (j + 1) * BLOCK)
-                hit = dest == wide + j * BLOCK
-                pick_ref[s, rows, cols] = jnp.where(hit, 1.0, 0.0).astype(jnp.bfloat16)
-                hit = constant_row(s, 1, j).astype(jnp.int32) == tall + band * BAND
-                drop_ref[s, rows, cols] = jnp.where(hit, 1.0, 0.0).astype(jnp.bfloat16)
+                there = wide + float(j * BLOCK)
+                edge_row = constant_row(edge_source, 1, j // 2, j % 2)
+                middle_row = constant_row(1, 1, j // 2, j % 2)
+                pick = jnp.where(edge_column == there, 1.0, 0.0)
+                drop = jnp.where(edge_row == here, 1.0, 0.0)
+                out_of_inner_ref[rows, cols] = jnp.where(first, pick, drop).astype(jnp.bfloat16)
+                in_of_outer_ref[rows, cols] = jnp.where(first, drop, pick).astype(jnp.bfloat16)
+                pick = jnp.where(middle_column == there, 1.0, 0.0)
+                drop = jnp.where(middle_row == here, 1.0, 0.0)
+                in_of_far_ref[rows, cols] = jnp.where(first, pick, drop).astype(jnp.bfloat16)
         return carry
 
     lax.fori_loop(0, bands, build, 0)
 
-    edge = jnp.zeros((BAND // TILE, TILE, BLOCK), jnp.float32)
-    for s in range(sections):
+    edge = jnp.zeros((tiles, TILE, BLOCK), jnp.float32)
+    for s in range(2):
         for slot in range(2):
             spread_ref[slot, s, 0] = edge
             spread_ref[slot, s, bands + 1] = edge
 
     def begin(band, carry):
-        rows = pl.ds(pl.multiple_of(band * BAND, BAND), BAND)
-        for s in range(sections):
+        rows = rows_of(band)
+        for s in range(2):
             field_ref[s, band, 0] = edge[0]
-            field_ref[s, band, BAND // TILE + 1] = edge[0]
-            value = start_of(s, band)
-            field_ref[s, band, 1 : BAND // TILE + 1] = value.reshape(BAND // TILE, TILE, BLOCK)
+            field_ref[s, band, tiles + 1] = edge[0]
+            value = loaded(sections[s], band, 0)
+            field_ref[s, band, 1 : tiles + 1] = value.reshape(tiles, TILE, BLOCK)
             pieces_ref[0, s, rows] = two_pieces(value)
-            pieces_ref[1, s, rows] = two_pieces(target_of(s, band))
-            velocity_ref[s, rows] = jnp.zeros((BAND, BLOCK), jnp.float32)
+            pieces_ref[1, s, rows] = two_pieces(loaded(sections[s], band, 1))
+            velocity_ref[s, band] = edge
             spread_band(0, s, band)
+        far_pieces_ref[rows] = two_pieces(loaded(far, band, 1))
         return carry
 
     lax.fori_loop(0, bands, begin, 0)
 
     ones = jnp.ones((total, BLOCK), jnp.bfloat16)
 
+    def product(matrix, values):
+        return jnp.dot(matrix, values, preferred_element_type=jnp.float32)
+
     def constants(band, carry):
-        rows = pl.ds(pl.multiple_of(band * BAND, BAND), BAND)
-        for s in range(sections):
-            weight = 8.0 * kappa_ref[s, rows]
-            force = jnp.zeros((BAND, BLOCK), jnp.float32)
-            if s < sections - 1:
-                alive = jnp.where(dest_ref[s, rows] >= 0, match_gain, 0.0)
-                weight = weight + alive
-                force = force + alive * target_of(s, band)
-            if s > 0:
-                drop = drop_ref[s - 1, rows]
-                count = jnp.dot(drop, ones, preferred_element_type=jnp.float32)
-                moved = jnp.dot(drop, pieces_ref[1, s - 1], preferred_element_type=jnp.float32)
-                weight = weight + match_gain * count
-                force = force - match_gain * joined(moved)
-            weight_ref[s, rows] = weight
-            force_ref[s, rows] = force
+        rows = rows_of(band)
+        out_rows, in_rows, far_rows = (
+            out_of_inner_ref[rows],
+            in_of_outer_ref[rows],
+            in_of_far_ref[rows],
+        )
+        count_out, count_in, count_far = (
+            product(matrix, ones) for matrix in (out_rows, in_rows, far_rows)
+        )
+        weight_ref[0, rows] = 8.0 * kappa_ref[0, rows] + match_gain * count_out
+        weight_ref[1, rows] = 8.0 * kappa_ref[1, rows] + match_gain * (count_in + count_far)
+        ahead = count_out * loaded(sections[0], band, 1)
+        behind = joined(product(out_rows, pieces_ref[1, 1]))
+        force_ref[0, rows] = match_gain * jnp.where(first, ahead, -behind)
+        alive = jnp.where(first, count_far, count_in)
+        from_outer = joined(product(in_rows, pieces_ref[1, 0]))
+        from_far = joined(product(far_rows, far_pieces_ref[...]))
+        behind = jnp.where(first, from_outer, from_far)
+        force_ref[1, rows] = match_gain * (alive * loaded(sections[1], band, 1) - behind)
         return carry
 
     lax.fori_loop(0, bands, constants, 0)
+
+    def far_start(band, carry):
+        far_pieces_ref[rows_of(band)] = two_pieces(loaded(far, band, 0))
+        return carry
+
+    lax.fori_loop(0, bands, far_start, 0)
+
+    def swap(slot, band):
+        return pltpu.make_async_remote_copy(
+            src_ref=field_ref.at[1, band, pl.ds(1, tiles)],
+            dst_ref=far_ref.at[slot, band],
+            send_sem=swap_send.at[band],
+            recv_sem=swap_recv.at[slot, band],
+            device_id=sibling,
+            device_id_type=pl.DeviceIdType.MESH,
+        )
+
+    def one_band(s, band, now, later):
+        rows = rows_of(band)
+        if s == 0:
+            sums = product(out_of_inner_ref[rows], pieces_ref[now, 1])
+        else:
+            sums = product(in_of_outer_ref[rows], pieces_ref[now, 0])
+            sums = sums + product(in_of_far_ref[rows], far_pieces_ref[...])
+        match_ref[...] = joined(sums)
+        base = pl.multiple_of(band * BAND, BAND)
+        for k in range(0, tiles, 2):
+            pair = []
+            for q in (k, k + 1):
+                spot = pl.ds(base + q * TILE, TILE)
+                here = spread_ref[now, s, band + 1, q]
+                above = spread_ref[now, s, band, q]
+                below = spread_ref[now, s, band + 2, q]
+                up = pltpu.roll(jnp.where(sub == TILE - 1, above, here), 1, 0)
+                down = pltpu.roll(jnp.where(sub == 0, below, here), TILE - 1, 0)
+                field = field_ref[s, band, q + 1]
+                velocity = (
+                    damping * velocity_ref[s, band, q]
+                    + kappa_ref[s, spot] * (2.0 * here + up + down)
+                    - weight_ref[s, spot] * field
+                    + match_gain * match_ref[q * TILE : (q + 1) * TILE]
+                    + force_ref[s, spot]
+                )
+                field = field + velocity
+                velocity_ref[s, band, q] = velocity
+                field_ref[s, band, q + 1] = field
+                pair.append(field)
+            spot = pl.ds(base + k * TILE, 2 * TILE)
+            pieces_ref[later, s, spot] = two_pieces(jnp.concatenate(pair, axis=0))
 
     def step(t, carry):
         now = lax.rem(t, 2)
         later = 1 - now
 
-        def one_section(s):
-            def one_band(band, inner):
-                rows = pl.ds(pl.multiple_of(band * BAND, BAND), BAND)
-                sums = None
-                if s < sections - 1:
-                    sums = jnp.dot(
-                        pick_ref[s, rows], pieces_ref[now, s + 1], preferred_element_type=jnp.float32
-                    )
-                if s > 0:
-                    other = jnp.dot(
-                        drop_ref[s - 1, rows],
-                        pieces_ref[now, s - 1],
-                        preferred_element_type=jnp.float32,
-                    )
-                    sums = other if sums is None else sums + other
-                match_ref[...] = joined(sums)
-                base = pl.multiple_of(band * BAND, BAND)
-                for k in range(0, BAND // TILE, 2):
-                    pair = []
-                    for q in (k, k + 1):
-                        spot = pl.ds(base + q * TILE, TILE)
-                        here = spread_ref[now, s, band + 1, q]
-                        above = spread_ref[now, s, band, q]
-                        below = spread_ref[now, s, band + 2, q]
-                        up = pltpu.roll(jnp.where(sub == TILE - 1, above, here), 1, 0)
-                        down = pltpu.roll(jnp.where(sub == 0, below, here), TILE - 1, 0)
-                        field = field_ref[s, band, q + 1]
-                        velocity = (
-                            damping * velocity_ref[s, spot]
-                            + kappa_ref[s, spot] * (2.0 * here + up + down)
-                            - weight_ref[s, spot] * field
-                            + match_gain * match_ref[q * TILE : (q + 1) * TILE]
-                            + force_ref[s, spot]
-                        )
-                        field = field + velocity
-                        velocity_ref[s, spot] = velocity
-                        field_ref[s, band, q + 1] = field
-                        pair.append(field)
-                    spot = pl.ds(base + k * TILE, 2 * TILE)
-                    pieces_ref[later, s, spot] = two_pieces(jnp.concatenate(pair, axis=0))
-                spread_band(later, s, band)
-                return inner
-
-            lax.fori_loop(0, bands, one_band, 0)
-
-        for s in range(sections):
-            distance = jnp.abs(section - s)
-
-            @pl.when(distance <= STEPS - 1 - t)
-            def _(s=s):
-                one_section(s)
-
+        def inner(band, inside):
+            one_band(1, band, now, later)
+            swap(now, band).start()
+            spread_band(later, 1, band)
+            return inside
+
+        def outer(band, inside):
+            one_band(0, band, now, later)
+            spread_band(later, 0, band)
+            return inside
+
+        lax.fori_loop(0, bands, inner, 0)
+        lax.fori_loop(0, bands, outer, 0)
+
+        def arrived(band, inside):
+            swap(now, band).wait()
+            value = far_ref[now, band].reshape(BAND, BLOCK)
+            far_pieces_ref[rows_of(band)] = two_pieces(value)
+            return inside
+
+        lax.fori_loop(0, bands, arrived, 0)
         return carry
 
-    lax.fori_loop(0, STEPS, step, 0)
-    for q in range(2):
-        band = half * 2 + q
-        out_ref[q, 0] = field_ref[section, band, 1 : BAND // TILE + 1].reshape(BAND, BLOCK)
-        out_ref[q, 1] = velocity_ref[section, pl.ds(pl.multiple_of(band * BAND, BAND), BAND)]
-
-
-def tiled_order(value):
-    lead = value.shape[:-2]
-    rows, cols = value.shape[-2:]
-    split = value.reshape(*lead, rows, cols // BLOCK, BLOCK)
-    return jnp.swapaxes(split, -3, -2).reshape(*lead, rows * (cols // BLOCK), BLOCK)
+    lax.fori_loop(0, STEPS - 1, step, 0)
+
+    now = (STEPS - 1) % 2
+    sends = core == x
+
+    def parts_of(s, band):
+        return (field_ref.at[s, band, pl.ds(1, tiles)], velocity_ref.at[s, band])
+
+    def deliver(s, band, peer, count):
+        return [
+            pltpu.make_async_remote_copy(
+                src_ref=source,
+                dst_ref=out_ref.at[comp, kind],
+                send_sem=out_send.at[count, kind],
+                recv_sem=out_recv.at[comp, kind],
+                device_id=peer,
+                device_id_type=pl.DeviceIdType.MESH,
+            )
+            for kind, source in enumerate(parts_of(s, band))
+        ]
+
+    def keep():
+        return [
+            pltpu.make_async_copy(source, out_ref.at[comp, kind], out_local.at[kind])
+            for kind, source in enumerate(parts_of(0, z))
+        ]
+
+    def landed(which):
+        return [
+            pltpu.make_async_remote_copy(
+                src_ref=out_ref.at[which, kind],
+                dst_ref=out_ref.at[which, kind],
+                send_sem=out_send.at[0, kind],
+                recv_sem=out_recv.at[which, kind],
+                device_id=sibling,
+                device_id_type=pl.DeviceIdType.MESH,
+            )
+            for kind in range(2)
+        ]
+
+    @pl.when(sends)
+    def _():
+        one_band(1, other_z, now, 1 - now)
+        for copy in deliver(1, other_z, across, 0):
+            copy.start()
+        one_band(0, other_z, now, 1 - now)
+        for copy in deliver(0, other_z, beside, 1):
+            copy.start()
+        one_band(1, z, now, 1 - now)
+        for copy in deliver(1, z, sibling, 2):
+            copy.start()
+        one_band(0, z, now, 1 - now)
+        for copy in keep():
+            copy.start()
+        for copy in deliver(1, other_z, across, 0):
+            copy.wait_send()
+        for copy in deliver(0, other_z, beside, 1):
+            copy.wait_send()
+        for copy in deliver(1, z, sibling, 2):
+            copy.wait_send()
+        for copy in keep():
+            copy.wait()
+
+    @pl.when(jnp.logical_not(sends))
+    def _():
+        for copy in landed(comp):
+            copy.wait_recv()
+
+    for copy in landed(1 - comp):
+        copy.wait_recv()
 
 
 def gather_kernel(bands, own_ref, data_ref, local_sem, send_sem, recv_sem):
@@ -439,31 +547,35 @@
             collective_id=0, has_side_effects=True, vmem_limit_bytes=16 * 1024 * 1024
         ),
     )(both)
-    place = jnp.stack([lax.axis_index("stack"), lax.axis_index("half")]).astype(jnp.int32)
     result = pl.pallas_call(
-        functools.partial(relax_kernel, sections, bands),
-        out_shape=jax.ShapeDtypeStruct((2, 2, BAND, BLOCK), jnp.float32),
-        in_specs=[
-            pl.BlockSpec(memory_space=pltpu.SMEM),
-            pl.BlockSpec(memory_space=pltpu.VMEM),
-        ],
+        functools.partial(relax_kernel, bands),
+        out_shape=jax.ShapeDtypeStruct((2, 2, tiles, TILE, BLOCK), jnp.float32),
+        in_specs=[pl.BlockSpec(memory_space=pltpu.VMEM)],
         out_specs=pl.BlockSpec(memory_space=pltpu.VMEM),
         scratch_shapes=[
-            pltpu.VMEM((sections, total, BLOCK), jnp.float32),
-            pltpu.VMEM((sections - 1, total, BLOCK), jnp.int32),
-            pltpu.VMEM((sections - 1, total, total), jnp.bfloat16),
-            pltpu.VMEM((sections - 1, total, total), jnp.bfloat16),
-            pltpu.VMEM((sections, bands, tiles + 2, TILE, BLOCK), jnp.float32),
-            pltpu.VMEM((sections, total, BLOCK), jnp.float32),
-            pltpu.VMEM((sections, total, BLOCK), jnp.float32),
-            pltpu.VMEM((sections, total, BLOCK), jnp.float32),
-            pltpu.VMEM((2, sections, total, 2 * BLOCK), jnp.bfloat16),
-            pltpu.VMEM((2, sections, bands + 2, tiles, TILE, BLOCK), jnp.float32),
+            pltpu.VMEM((2, total, BLOCK), jnp.float32),
+            pltpu.VMEM((total, total), jnp.bfloat16),
+            pltpu.VMEM((total, total), jnp.bfloat16),
+            pltpu.VMEM((total, total), jnp.bfloat16),
+            pltpu.VMEM((2, bands, tiles + 2, TILE, BLOCK), jnp.float32),
+            pltpu.VMEM((2, bands, tiles, TILE, BLOCK), jnp.float32),
+            pltpu.VMEM((2, total, BLOCK), jnp.float32),
+            pltpu.VMEM((2, total, BLOCK), jnp.float32),
+            pltpu.VMEM((2, 2, total, 2 * BLOCK), jnp.bfloat16),
+            pltpu.VMEM((total, 2 * BLOCK), jnp.bfloat16),
+            pltpu.VMEM((2, bands, tiles, TILE, BLOCK), jnp.float32),
+            pltpu.VMEM((2, 2, bands + 2, tiles, TILE, BLOCK), jnp.float32),
             pltpu.VMEM((BAND, BLOCK), jnp.float32),
+            pltpu.SemaphoreType.DMA((bands,)),
+            pltpu.SemaphoreType.DMA((2, bands)),
+            pltpu.SemaphoreType.DMA((3, 2)),
+            pltpu.SemaphoreType.DMA((2, 2)),
+            pltpu.SemaphoreType.DMA((2,)),
         ],
-        compiler_params=pltpu.CompilerParams(vmem_limit_bytes=VMEM_BYTES),
-    )(place, data)
-    result = lax.all_to_all(result, "comp", split_axis=0, concat_axis=0, tiled=True)
+        compiler_params=pltpu.CompilerParams(
+            collective_id=1, has_side_effects=True, vmem_limit_bytes=VMEM_BYTES
+        ),
+    )(data)
     result = result.reshape(2, 2, tiles, TILE, BLOCK).transpose(1, 0, 3, 2, 4)
     result = result.reshape(2, 1, 2, TILE, tiles * BLOCK)
     return (result[0], result[1])

time: 125 us -> 99.8 us (0.80)
  the two profiles are of different devices: /device:TPU:1 before, /device:TPU:0 now
where the time goes in v2:
time: 99.8 us; the launch traced here: 99.5 us
  Pallas kernels  92.2 us (92%)
  local copies, waits for them, and re-layouts  4.01 us (4%)
  other arithmetic  2.61 us (3%)
    pallas_call x1, Pallas kernels, whole_component(): pl.pallas_call(functools.partial(relax_kernel, bands), out_shape=jax.Shap...  55.4 us
    pallas_call x1, Pallas kernels, whole_component(): pl.pallas_call(functools.partial(gather_kernel, bands), out_shape=jax.Sha...  36.8 us

profile of v2, /device:TPU:0, one launch (start us, length us, event | category | flops | bytes accessed | tf_op | source)
XLA Modules:
  0.0 99.5 jit_solution(16868076957977805944)
XLA Ops:
  0.6 0.8 select_reduce_fusion
  1.4 0.7 fusion.5
  2.1 0.1 copy.14
  2.2 0.1 reshape.23
  2.3 1.1 %maximum_bitcast_fusion = f32[2,2,256,128]{3,2,1,0:T(8,128)S(1)} fusion(f32[2,1,8,32,128]{4,2,3,1,0:T(8,128)} %bitcast.43, f32[2,1,8,32,128]{4,2,3,1,0:T(8,128)} %bitcast.44), kind=kLoop, calls=%fused_computation.1 | loop fusion | flops 131072 | bytes 1048576 | tf_op jit(solution)/shard_map/reshape | solution.py:514
  3.5 36.8 %shard_map.68.data_ref = f32[2,2,4,2,264,128]{5,4,3,2,1,0:T(8,128)S(1)} custom-call(f32[2,2,264,128]{3,2,1,0:T(8,128)S(1)} %pad_maximum_fusion.own_ref), custom_call_target="tpu_custom_call" | custom-call | tf_op jit(solution)/shard_map/pallas_call | solution.py:534
  40.2 0.0 copy-start
  40.3 2.0 %copy-done = f32[2,2,4,2,264,128]{5,4,3,2,1,0:T(8,128)} copy-done((f32[2,2,4,2,264,128]{5,4,3,2,1,0:T(8,128)}, f32[2,2,4,2,264,128]{5,4,3,2,1,0:T(8,128)S(1)}, u32[]{:S(2)}) %copy-start) | copy-done | bytes 4325400
  42.2 55.4 %shard_map.69 = f32[2,2,32,8,128]{4,3,2,1,0:T(8,128)} custom-call(f32[2,2,4,2,264,128]{5,4,3,2,1,0:T(8,128)} %copy-done), custom_call_target="tpu_custom_call" | custom-call | tf_op jit(solution)/shard_map/pallas_call | solution.py:550
  97.7 1.9 %slice_bitcast_fusion = (f32[1,2,8,4096]{3,2,1,0:T(8,128)}, f32[1,2,8,4096]{3,2,1,0:T(8,128)}) fusion(f32[2,2,8,32,128]{4,2,3,0,1:T(8,128)} %bitcast.42), kind=kLoop, calls=%fused_computation.2 | loop fusion | bytes 1048576 | tf_op jit(solution)/shard_map/squeeze | solution.py:581
  (4 shorter events, 0.1 us)
Async XLA Ops:
  40.2 2.0 %copy-start = (f32[2,2,4,2,264,128]{5,4,3,2,1,0:T(8,128)}, f32[2,2,4,2,264,128]{5,4,3,2,1,0:T(8,128)S(1)}, u32[]{:S(2)}) copy-start(f32[2,2,4,2,264,128]{5,4,3,2,1,0:T(8,128)S(1)} %shard_map.68.data_ref) | copy-start | bytes 12976132

commit v3 on v2

--- a/solution.py
+++ b/solution.py
@@ -143,8 +143,9 @@
 
 def relax_kernel(
     bands,
+    own_ref,
+    out_ref,
     data_ref,
-    out_ref,
     kappa_ref,
     out_of_inner_ref,
     in_of_outer_ref,
@@ -163,6 +164,9 @@
     out_send,
     out_recv,
     out_local,
+    local_sem,
+    send_sem,
+    recv_sem,
 ):
     total = bands * BAND
     tiles = BAND // TILE
@@ -178,9 +182,74 @@
     beside = (slab, half, 1 - comp, x * 2 + core)
     across = (slab, half, 1 - comp, x * 2 + 1 - core)
     barrier = pltpu.get_barrier_semaphore()
-    for peer in (sibling, beside, across):
+    over_x = (slab, half, comp, (1 - x) * 2 + core)
+    along = [other_z, 2 - half, 3 - 3 * half]
+
+    def column(to_z):
+        return (slab, to_z // 2, to_z % 2, stack)
+
+    for peer in [column(to_z) for to_z in along] + [sibling, across, over_x]:
         pl.semaphore_signal(barrier, inc=1, device_id=peer, device_id_type=pl.DeviceIdType.MESH)
-    pl.semaphore_wait(barrier, 3)
+    pl.semaphore_wait(barrier, 6)
+
+    started = []
+
+    def send(source, slot, peer):
+        copy = pltpu.make_async_remote_copy(
+            src_ref=source,
+            dst_ref=data_ref.at[slot],
+            send_sem=send_sem.at[len(started)],
+            recv_sem=recv_sem.at[slot],
+            device_id=peer,
+            device_id_type=pl.DeviceIdType.MESH,
+        )
+        copy.start()
+        started.append(copy)
+
+    def arrive(slot):
+        pltpu.make_async_remote_copy(
+            src_ref=data_ref.at[slot],
+            dst_ref=data_ref.at[slot],
+            send_sem=send_sem.at[0],
+            recv_sem=recv_sem.at[slot],
+            device_id=sibling,
+            device_id_type=pl.DeviceIdType.MESH,
+        ).wait_recv()
+
+    kept = []
+    for kind in range(2):
+        for to_z in along:
+            send(own_ref.at[to_z % 2, kind], (x, core, z, kind), column(to_z))
+        send(own_ref.at[comp, kind], (x, core, z, kind), over_x)
+        copy = pltpu.make_async_copy(
+            own_ref.at[comp, kind], data_ref.at[x, core, z, kind], local_sem.at[kind]
+        )
+        copy.start()
+        kept.append(copy)
+    for copy in kept:
+        copy.wait()
+
+    def forward_column(kind):
+        for band in along:
+            slot = (x, core, band, kind)
+            arrive(slot)
+            send(data_ref.at[slot], slot, over_x)
+
+    def forward_sibling(kind):
+        for band in [z] + along:
+            arrive((1 - x, core, band, kind))
+        for band in [z] + along:
+            slot = (1 - core, core, band, kind)
+            send(data_ref.at[slot], slot, sibling)
+
+    def from_sibling(kind):
+        for band in [z] + along:
+            arrive((core, 1 - core, band, kind))
+
+    forward_column(0)
+    forward_sibling(0)
+    forward_column(1)
+    from_sibling(0)
 
     lane = lax.broadcasted_iota(jnp.int32, (TILE, BLOCK), 1)
     sub = lax.broadcasted_iota(jnp.int32, (TILE, BLOCK), 0)
@@ -250,13 +319,23 @@
             value = loaded(sections[s], band, 0)
             field_ref[s, band, 1 : tiles + 1] = value.reshape(tiles, TILE, BLOCK)
             pieces_ref[0, s, rows] = two_pieces(value)
-            pieces_ref[1, s, rows] = two_pieces(loaded(sections[s], band, 1))
             velocity_ref[s, band] = edge
             spread_band(0, s, band)
+        return carry
+
+    lax.fori_loop(0, bands, begin, 0)
+
+    forward_sibling(1)
+    from_sibling(1)
+
+    def offsets(band, carry):
+        rows = rows_of(band)
+        for s in range(2):
+            pieces_ref[1, s, rows] = two_pieces(loaded(sections[s], band, 1))
         far_pieces_ref[rows] = two_pieces(loaded(far, band, 1))
         return carry
 
-    lax.fori_loop(0, bands, begin, 0)
+    lax.fori_loop(0, bands, offsets, 0)
 
     ones = jnp.ones((total, BLOCK), jnp.bfloat16)
 
@@ -433,78 +512,8 @@
 
     for copy in landed(1 - comp):
         copy.wait_recv()
-
-
-def gather_kernel(bands, own_ref, data_ref, local_sem, send_sem, recv_sem):
-    half, comp, stack = (lax.axis_index(name) for name in ("half", "comp", "stack"))
-    slab = lax.axis_index("slab")
-    z = half * 2 + comp
-    x, core = stack // 2, stack % 2
-
-    def device(to_x, to_core, to_z):
-        return (slab, to_z // 2, to_z % 2, to_x * 2 + to_core)
-
-    along = [lax.rem(z + j, bands) for j in range(bands)]
-    over_x = device(1 - x, core, z)
-    sibling = device(x, 1 - core, z)
-    barrier = pltpu.get_barrier_semaphore()
-    for peer in [device(x, core, to_z) for to_z in along[1:]] + [over_x, sibling]:
-        pl.semaphore_signal(barrier, inc=1, device_id=peer, device_id_type=pl.DeviceIdType.MESH)
-    pl.semaphore_wait(barrier, bands + 1)
-
-    started = []
-
-    def send(source, slot, kind, peer):
-        copy = pltpu.make_async_remote_copy(
-            src_ref=source,
-            dst_ref=data_ref.at[slot],
-            send_sem=send_sem.at[len(started)],
-            recv_sem=recv_sem.at[slot],
-            device_id=peer,
-            device_id_type=pl.DeviceIdType.MESH,
-        )
-        copy.start()
-        started.append(copy)
-
-    def arrive(slot):
-        pltpu.make_async_remote_copy(
-            src_ref=data_ref.at[slot],
-            dst_ref=data_ref.at[slot],
-            send_sem=send_sem.at[0],
-            recv_sem=recv_sem.at[slot],
-            device_id=sibling,
-            device_id_type=pl.DeviceIdType.MESH,
-        ).wait_recv()
-
-    for kind in range(2):
-        for to_z in along[1:]:
-            send(own_ref.at[to_z % 2, kind], (x, core, z, kind), kind, device(x, core, to_z))
-        send(own_ref.at[comp, kind], (x, core, z, kind), kind, over_x)
-        send(own_ref.at[comp, kind], (x, core, z, kind), kind, sibling)
-        keep = pltpu.make_async_copy(
-            own_ref.at[comp, kind], data_ref.at[x, core, z, kind], local_sem.at[kind]
-        )
-        keep.start()
-    for kind in range(2):
-        for band in along[1:]:
-            slot = (x, core, band, kind)
-            arrive(slot)
-            send(data_ref.at[slot], slot, kind, over_x)
-            send(data_ref.at[slot], slot, kind, sibling)
-        for band in along:
-            slot = (1 - x, core, band, kind)
-            arrive(slot)
-            send(data_ref.at[slot], slot, kind, sibling)
-    for kind in range(2):
-        for band in along:
-            for from_x in range(2):
-                arrive((from_x, 1 - core, band, kind))
     for copy in started:
         copy.wait_send()
-    for kind in range(2):
-        pltpu.make_async_copy(
-            own_ref.at[comp, kind], data_ref.at[x, core, z, kind], local_sem.at[kind]
-        ).wait()
 
 
 def tiled_order(value):
@@ -530,29 +539,13 @@
     both = tiled_order(jnp.stack([disp[0], targets[0]], axis=1))
     extra = jnp.broadcast_to(constants, (2, 2, TILE, BLOCK))
     both = jnp.concatenate([both, extra], axis=2)
-    copies = 2 * (bands + 1) + 2 * (2 * (bands - 1) + bands)
-    data = pl.pallas_call(
-        functools.partial(gather_kernel, bands),
-        out_shape=jax.ShapeDtypeStruct(
-            (sections // 2, 2, bands, 2, BAND + TILE, BLOCK), jnp.float32
-        ),
-        in_specs=[pl.BlockSpec(memory_space=pltpu.VMEM)],
-        out_specs=pl.BlockSpec(memory_space=pltpu.VMEM),
-        scratch_shapes=[
-            pltpu.SemaphoreType.DMA((2,)),
-            pltpu.SemaphoreType.DMA((copies,)),
-            pltpu.SemaphoreType.DMA((sections // 2, 2, bands, 2)),
-        ],
-        compiler_params=pltpu.CompilerParams(
-            collective_id=0, has_side_effects=True, vmem_limit_bytes=16 * 1024 * 1024
-        ),
-    )(both)
     result = pl.pallas_call(
         functools.partial(relax_kernel, bands),
         out_shape=jax.ShapeDtypeStruct((2, 2, tiles, TILE, BLOCK), jnp.float32),
         in_specs=[pl.BlockSpec(memory_space=pltpu.VMEM)],
         out_specs=pl.BlockSpec(memory_space=pltpu.VMEM),
         scratch_shapes=[
+            pltpu.VMEM((sections // 2, 2, bands, 2, BAND + TILE, BLOCK), jnp.float32),
             pltpu.VMEM((2, total, BLOCK), jnp.float32),
             pltpu.VMEM((total, total), jnp.bfloat16),
             pltpu.VMEM((total, total), jnp.bfloat16),
@@ -571,11 +564,14 @@
             pltpu.SemaphoreType.DMA((3, 2)),
             pltpu.SemaphoreType.DMA((2, 2)),
             pltpu.SemaphoreType.DMA((2,)),
+            pltpu.SemaphoreType.DMA((2,)),
+            pltpu.SemaphoreType.DMA((22,)),
+            pltpu.SemaphoreType.DMA((sections // 2, 2, bands, 2)),
         ],
         compiler_params=pltpu.CompilerParams(
-            collective_id=1, has_side_effects=True, vmem_limit_bytes=VMEM_BYTES
+            collective_id=0, has_side_effects=True, vmem_limit_bytes=VMEM_BYTES
         ),
-    )(data)
+    )(both)
     result = result.reshape(2, 2, tiles, TILE, BLOCK).transpose(1, 0, 3, 2, 4)
     result = result.reshape(2, 1, 2, TILE, tiles * BLOCK)
     return (result[0], result[1])
@@ -583,7 +579,7 @@
 
 def solution(mesh):
     by_name = mesh.shape
-    if by_name["grid"] % 2 == 0 and by_name["grid"] <= 4 and by_name["stack"] == 4:
+    if by_name["grid"] == 4 and by_name["stack"] == 4:
         inner = Mesh(
             mesh.devices.reshape(by_name["slab"], by_name["grid"] // 2, 2, by_name["stack"]),
             ("slab", "half", "comp", "stack"),

time: 99.8 us -> 87.3 us (0.87)
  Pallas kernels: 92.2 us -> 81 us
    pallas_call x1 -> x0, Pallas kernels: 36.8 us -> none  [whole_component(): pl.pallas_call(functools.partial(gather_kernel, bands), out_shape=jax.Sha...]
    pallas_call x1, Pallas kernels: 55.4 us -> 81 us  [whole_component(): pl.pallas_call(functools.partial(relax_kernel, bands), out_shape=jax.Shap...]
where the time goes in v3:
time: 87.3 us; the launch traced here: 87 us
  Pallas kernels  81 us (93%)
  local copies, waits for them, and re-layouts  3.32 us (4%)
  other arithmetic  2.01 us (2%)
    pallas_call x1, Pallas kernels, whole_component(): pl.pallas_call(functools.partial(relax_kernel, bands), out_shape=jax.Shap...  81 us
    squeeze x1, local copies, waits for them, and re-layouts, whole_component(): return (result[0], result[1])  1.86 us

profile of v3, /device:TPU:0, one launch (start us, length us, event | category | flops | bytes accessed | tf_op | source)
XLA Modules:
  0.0 87.0 jit_solution(13832372442566263679)
XLA Ops:
  0.6 0.0 copy-start
  0.6 0.0 copy-start.2
  0.7 0.7 copy-done
  1.3 0.0 copy-done.2
  1.3 0.0 copy-start.1
  1.3 0.1 select_reduce_fusion
  1.4 0.6 copy-done.1
  2.0 0.1 copy.14
  2.1 0.1 reshape.23
  2.2 1.1 %maximum_bitcast_fusion = f32[2,2,256,128]{3,2,1,0:T(8,128)S(1)} fusion(f32[2,1,8,32,128]{4,2,3,1,0:T(8,128)} %bitcast.43, f32[2,1,8,32,128]{4,2,3,1,0:T(8,128)} %bitcast.44), kind=kLoop, calls=%fused_computation.1 | loop fusion | flops 131072 | bytes 1048576 | tf_op jit(solution)/shard_map/reshape | solution.py:523
  3.3 0.8 pad_maximum_fusion.own_ref
  4.2 81.0 %shard_map.68 = f32[2,2,32,8,128]{4,3,2,1,0:T(8,128)} custom-call(f32[2,2,264,128]{3,2,1,0:T(8,128)} %pad_maximum_fusion.own_ref), custom_call_target="tpu_custom_call" | custom-call | tf_op jit(solution)/shard_map/pallas_call | solution.py:542
  85.1 1.9 %slice_bitcast_fusion = (f32[1,2,8,4096]{3,2,1,0:T(8,128)}, f32[1,2,8,4096]{3,2,1,0:T(8,128)}) fusion(f32[2,2,8,32,128]{4,2,3,0,1:T(8,128)} %bitcast.42), kind=kLoop, calls=%fused_computation.2 | loop fusion | bytes 1048576 | tf_op jit(solution)/shard_map/squeeze | solution.py:577
  (4 shorter events, 0.0 us)
Async XLA Ops:
  0.6 0.7 copy-start
  0.6 0.7 copy-start.2
  1.3 0.7 copy-start.1

commit v4 on v3

--- a/solution.py
+++ b/solution.py
@@ -265,6 +265,8 @@
         return jnp.broadcast_to(row, (BLOCK, BLOCK)).T
 
     def rows_of(band):
+        if isinstance(band, int):
+            return slice(band * BAND, (band + 1) * BAND)
         return pl.ds(pl.multiple_of(band * BAND, BAND), BAND)
 
     def spread_band(slot, s, band):
@@ -382,15 +384,17 @@
             device_id_type=pl.DeviceIdType.MESH,
         )
 
-    def one_band(s, band, now, later):
+    def match_band(s, band, now, buffer):
         rows = rows_of(band)
         if s == 0:
             sums = product(out_of_inner_ref[rows], pieces_ref[now, 1])
         else:
             sums = product(in_of_outer_ref[rows], pieces_ref[now, 0])
             sums = sums + product(in_of_far_ref[rows], far_pieces_ref[...])
-        match_ref[...] = joined(sums)
-        base = pl.multiple_of(band * BAND, BAND)
+        match_ref[buffer] = joined(sums)
+
+    def move_band(s, band, now, later, buffer):
+        base = band * BAND if isinstance(band, int) else pl.multiple_of(band * BAND, BAND)
         for k in range(0, tiles, 2):
             pair = []
             for q in (k, k + 1):
@@ -405,7 +409,7 @@
                     damping * velocity_ref[s, band, q]
                     + kappa_ref[s, spot] * (2.0 * here + up + down)
                     - weight_ref[s, spot] * field
-                    + match_gain * match_ref[q * TILE : (q + 1) * TILE]
+                    + match_gain * match_ref[buffer, q * TILE : (q + 1) * TILE]
                     + force_ref[s, spot]
                 )
                 field = field + velocity
@@ -415,23 +419,22 @@
             spot = pl.ds(base + k * TILE, 2 * TILE)
             pieces_ref[later, s, spot] = two_pieces(jnp.concatenate(pair, axis=0))
 
-    def step(t, carry):
-        now = lax.rem(t, 2)
+    def one_band(s, band, now, later):
+        match_band(s, band, now, 0)
+        move_band(s, band, now, later, 0)
+
+    tasks = [(s, band) for s in (1, 0) for band in range(bands)]
+
+    def step(now):
         later = 1 - now
-
-        def inner(band, inside):
-            one_band(1, band, now, later)
-            swap(now, band).start()
-            spread_band(later, 1, band)
-            return inside
-
-        def outer(band, inside):
-            one_band(0, band, now, later)
-            spread_band(later, 0, band)
-            return inside
-
-        lax.fori_loop(0, bands, inner, 0)
-        lax.fori_loop(0, bands, outer, 0)
+        match_band(*tasks[0], now, 0)
+        for turn, (s, band) in enumerate(tasks):
+            if turn + 1 < len(tasks):
+                match_band(*tasks[turn + 1], now, (turn + 1) % 2)
+            move_band(s, band, now, later, turn % 2)
+            if s == 1:
+                swap(now, band).start()
+            spread_band(later, s, band)
 
         def arrived(band, inside):
             swap(now, band).wait()
@@ -440,9 +443,15 @@
             return inside
 
         lax.fori_loop(0, bands, arrived, 0)
+
+    def two_steps(t, carry):
+        step(0)
+        step(1)
         return carry
 
-    lax.fori_loop(0, STEPS - 1, step, 0)
+    lax.fori_loop(0, (STEPS - 1) // 2, two_steps, 0)
+    if STEPS % 2 == 0:
+        step(0)
 
     now = (STEPS - 1) % 2
     sends = core == x
@@ -558,7 +567,7 @@
             pltpu.VMEM((total, 2 * BLOCK), jnp.bfloat16),
             pltpu.VMEM((2, bands, tiles, TILE, BLOCK), jnp.float32),
             pltpu.VMEM((2, 2, bands + 2, tiles, TILE, BLOCK), jnp.float32),
-            pltpu.VMEM((BAND, BLOCK), jnp.float32),
+            pltpu.VMEM((2, BAND, BLOCK), jnp.float32),
             pltpu.SemaphoreType.DMA((bands,)),
             pltpu.SemaphoreType.DMA((2, bands)),
             pltpu.SemaphoreType.DMA((3, 2)),

time: 87.3 us -> 85.4 us (0.978)
  Pallas kernels: 81 us -> 79.1 us
    pallas_call x1, Pallas kernels: 81 us -> 79.1 us  [whole_component(): pl.pallas_call(functools.partial(relax_kernel, bands), out_shape=jax.Shap...]
where the time goes in v4:
time: 85.4 us; the launch traced here: 85.1 us
  Pallas kernels  79.1 us (93%)
  local copies, waits for them, and re-layouts  3.32 us (4%)
  other arithmetic  2.01 us (2%)
    pallas_call x1, Pallas kernels, whole_component(): pl.pallas_call(functools.partial(relax_kernel, bands), out_shape=jax.Shap...  79.1 us
    squeeze x1, local copies, waits for them, and re-layouts, whole_component(): return (result[0], result[1])  1.86 us

profile of v4, /device:TPU:0, one launch (start us, length us, event | category | flops | bytes accessed | tf_op | source)
XLA Modules:
  0.0 85.1 jit_solution(10173450681823161788)
XLA Ops:
  0.6 0.0 copy-start
  0.6 0.0 copy-start.2
  0.7 0.7 copy-done
  1.3 0.0 copy-done.2
  1.3 0.0 copy-start.1
  1.3 0.1 select_reduce_fusion
  1.4 0.6 copy-done.1
  2.0 0.1 copy.14
  2.1 0.1 reshape.23
  2.2 1.1 %maximum_bitcast_fusion = f32[2,2,256,128]{3,2,1,0:T(8,128)S(1)} fusion(f32[2,1,8,32,128]{4,2,3,1,0:T(8,128)} %bitcast.43, f32[2,1,8,32,128]{4,2,3,1,0:T(8,128)} %bitcast.44), kind=kLoop, calls=%fused_computation.1 | loop fusion | flops 131072 | bytes 1048576 | tf_op jit(solution)/shard_map/reshape | solution.py:532
  3.3 0.8 pad_maximum_fusion.own_ref
  4.2 79.1 %shard_map.68 = f32[2,2,32,8,128]{4,3,2,1,0:T(8,128)} custom-call(f32[2,2,264,128]{3,2,1,0:T(8,128)} %pad_maximum_fusion.own_ref), custom_call_target="tpu_custom_call" | custom-call | tf_op jit(solution)/shard_map/pallas_call | solution.py:551
  83.3 1.9 %slice_bitcast_fusion = (f32[1,2,8,4096]{3,2,1,0:T(8,128)}, f32[1,2,8,4096]{3,2,1,0:T(8,128)}) fusion(f32[2,2,8,32,128]{4,2,3,0,1:T(8,128)} %bitcast.42), kind=kLoop, calls=%fused_computation.2 | loop fusion | bytes 1048576 | tf_op jit(solution)/shard_map/squeeze | solution.py:586
  (4 shorter events, 0.0 us)
Async XLA Ops:
  0.6 0.7 copy-start
  0.6 0.7 copy-start.2
  1.3 0.7 copy-start.1
